TPU v7x, 32 devices: a whole 2x2x4 slice. The times are simulated.
32 devices in a mesh: ep: 16 (over z, y, core), dp: 2 (over x).
Axes of the slice: x: 2, y: 2, z: 4, core: 2. Of those that a mesh axis runs over, the one named last changes fastest.
Arguments:
- gradients: float32 [2, 2048, 7168], P('dp', 'ep'), may hold values from -18 to 18
- master_rows: float32 [16, 192, 7168], P('ep', 'dp'), may hold values from -0.24 to 0.24
- first_moment: float32 [16, 192, 7168], P('ep', 'dp'), may hold values from -2 to 2
- second_moment: float32 [16, 192, 7168], P('ep', 'dp'), may hold values from 0.1 to 1
- shard_rows: int32 [16, 2], replicated, may hold values from 1 to 96, as said below
- move_partner: int32 [16], replicated, may hold values from 0 to 15, as said below
Outputs:
- new_master: float32 [16, 192, 7168], P('ep', 'dp')
- new_first: float32 [16, 192, 7168], P('ep', 'dp')
- new_second: float32 [16, 192, 7168], P('ep', 'dp')
- placed_params: bfloat16 [2048, 7168], P('ep')
Inputs may be any that keep to these rules, and one draw needn't show every extreme that they name: `shard_rows`: in each row the shards own consecutive runs of the 128 flat rows in order, each at least one row, summing to 128; the largest of each row is exactly 96. move_partner[i] is i or i with one binary digit flipped; that digit is the same for every i that moves; move_partner[move_partner[i]] == i.
All inputs are finite; a program needn't handle non-finite values.
Results may differ from a plain program's by a relative error of at most 0.014.
Values may be sent and summed in bfloat16 or wider, within the bound.
A program may use at most 128 MiB of HBM per device.

v0:
```python
import functools

import jax
import jax.numpy as jnp
from jax import lax
from jax.experimental import pallas as pl
from jax.experimental.pallas import tpu as pltpu
from jax.sharding import PartitionSpec as P

beta_one = 0.9
beta_two = 0.95
learn_rate = 0.02
weight_decay = 0.1
epsilon = 1e-08
shifts_of_bit = ((0,), (16, 32), (16, 32), (32,))
correct_one = 1.0 - 0.9**10
correct_two = 1.0 - 0.95**10


def swapped(array, axis, apart):
    return lax.ppermute(array, axis, [(i, i ^ 1 << apart) for i in range(lax.axis_size(axis))])


def adam_step(grad_rows, weights, first, second):
    first_new = beta_one * first + (1.0 - beta_one) * grad_rows
    second_new = beta_two * second + (1.0 - beta_two) * grad_rows * grad_rows
    ratio = first_new / correct_one / (jnp.sqrt(second_new / correct_two) + epsilon)
    updated = weights - learn_rate * (ratio + weight_decay * weights)
    return updated, first_new, second_new


def chosen_case(move_partner):
    count = move_partner.shape[0]
    flips = jnp.bitwise_xor(move_partner, jnp.arange(count, dtype=jnp.int32))
    digit = jnp.max(flips)
    return sum((digit >= 1 << bit).astype(jnp.int32) for bit in range(1, count.bit_length() - 1))


def move_new(values, partner, ep_index, move_partner):
    bits = lax.axis_size("ep").bit_length() - 1

    def exchange(bit_index):
        def run(values):
            arrived = swapped(values.astype(jnp.bfloat16), "ep", bit_index)
            return jnp.where(partner == ep_index, values, arrived.astype(values.dtype))
        return run

    return lax.switch(
        chosen_case(move_partner), [exchange(bit_index) for bit_index in range(bits)], values
    )


def fused_kernel(
    bit, shifts, lag, counts_ref, partner_ref, grad_hbm, master_hbm, first_hbm, second_hbm,
    new_hbm, placed_hbm,
    grad, state, edge_out, edge_in, mid_out, mid_in, own_out, own_in, slot_out, slot_in,
    back_out, back_in, new, placed,
    load_sem, edge_send, edge_recv, mid_send, mid_recv, own_send, own_recv, rest_send, rest_recv,
    slot_send, slot_recv, back_send, back_recv, new_sem, placed_sem,
):
    parts, _, width = own_out.shape
    flat_count, capacity = grad.shape[0], state.shape[1]
    edge = flat_count - capacity
    middle = flat_count - 2 * edge
    trail = 4
    deferred = parts - (6 if bit else 0)
    low, high = jnp.bfloat16, jnp.float32
    ep_index, dp_index = lax.axis_index("ep"), lax.axis_index("dp")
    step = 1 << bit
    mate = ep_index + step * (1 - 2 * ((ep_index // step) % 2))
    to_peer, to_mate = {"dp": 1 - dp_index}, {"ep": mate}
    mesh_ids = pl.DeviceIdType.MESH

    def columns(part):
        return pl.ds(pl.multiple_of(part * width, width), width)

    def load(index):
        source = (grad_hbm, master_hbm, first_hbm, second_hbm)[index]
        target = grad if index == 0 else state.at[index - 1]
        return pltpu.make_async_copy(source, target, load_sem.at[index])

    def remote(part, rows, out, into, sent, received, target):
        return pltpu.make_async_remote_copy(
            out.at[part, :rows], into.at[part, :rows], sent.at[part], received.at[part],
            device_id=target, device_id_type=mesh_ids)

    def send_edge(part):
        return remote(part, edge, edge_out, edge_in, edge_send, edge_recv, to_peer)

    def send_mid(part, shifted):
        rows = max(middle, 3 * shifted)
        return remote(part, rows, mid_out, mid_in, mid_send, mid_recv, to_peer)

    def send_own(part, rows):
        return remote(part, rows, own_out, own_in, own_send, own_recv, to_mate)

    def send_rest(part):
        return pltpu.make_async_remote_copy(
            own_out.at[part, edge:], own_in.at[part, edge:], rest_send.at[part],
            rest_recv.at[part], device_id=to_mate, device_id_type=mesh_ids)

    def either(part, step_of):
        @pl.when(part < deferred)
        def _():
            step_of(3 * edge)

        @pl.when(part >= deferred)
        def _():
            step_of(edge)

    def send_slot(part, shifted):
        rows = 3 * max(middle - shifted, shifted)
        return remote(part, rows, slot_out, slot_in, slot_send, slot_recv, to_mate)

    def send_back(part, shifted):
        rows = edge + (max(middle - shifted, 3 * shifted) if shifted else 0)
        return remote(part, rows, back_out, back_in, back_send, back_recv, to_peer)

    def store_new(part):
        return pltpu.make_async_copy(new.at[part], new_hbm.at[:, :, columns(part)], new_sem.at[part])

    def store_placed(part):
        return pltpu.make_async_copy(
            placed.at[part], placed_hbm.at[:, columns(part)], placed_sem.at[part])

    def each(count, step_of):
        def run(group, carry):
            for index, shifted in enumerate(shifts):
                step_of(group * len(shifts) + index, shifted)
            return carry
        lax.fori_loop(0, -(-count // len(shifts)), run, 0)

    barrier = pltpu.get_barrier_semaphore()
    pl.semaphore_signal(barrier, inc=1, device_id=to_peer, device_id_type=mesh_ids)
    pl.semaphore_signal(barrier, inc=1, device_id=to_mate, device_id_type=mesh_ids)
    for index in range(4):
        load(index).start()
    pl.semaphore_wait(barrier, 2)

    source = partner_ref[ep_index]
    owns_value = counts_ref[ep_index, dp_index]
    moves_value = source
    owns_moved_value = counts_ref[source, dp_index]

    def full(value, rows):
        return jnp.broadcast_to(value, (rows, width))

    def owns(rows):
        return full(owns_value, rows) == capacity

    def owns_moved(rows):
        return full(owns_moved_value, rows) == capacity

    def moves(rows):
        return full(moves_value, rows) != ep_index

    def is_last(rows):
        return full(dp_index, rows) == 1

    def select(mask, one, other):
        return jnp.where(mask, one.astype(high), other.astype(high))

    own_edge = pl.ds(pl.multiple_of((flat_count - edge) * dp_index, edge), edge)
    peer_edge = pl.ds(pl.multiple_of((flat_count - edge) * (1 - dp_index), edge), edge)
    own_middle = pl.ds(pl.multiple_of(edge * (1 - dp_index), edge), middle)

    def update_edge(part):
        send_edge(part).wait_recv()
        held = columns(part)

        @pl.when(part == 0)
        def _():
            for index in range(1, 4):
                load(index).wait()

        edge_mean = (grad[own_edge, held] + edge_in[part].astype(high)) / 2
        late = jnp.logical_and(owns(edge), is_last(edge))
        edge_state = [
            jnp.where(late, state[index, capacity - edge:, held], state[index, :edge, held])
            for index in range(3)
        ]
        for index, result in enumerate(adam_step(edge_mean, *edge_state)):
            own_out[part, index * edge:(index + 1) * edge] = result.astype(low)
        either(part, lambda rows: send_own(part, rows).start())

    def update_middle(part, shifted):
        kept = middle - shifted
        slot_rows = max(kept, shifted)
        middle_mean = (
            grad[edge:edge + middle, columns(part)] + mid_in[part, :middle].astype(high)) / 2
        middle_state = [state[index, own_middle, columns(part)] for index in range(3)]
        for index, result in enumerate(adam_step(middle_mean, *middle_state)):
            result = result.astype(low)
            slot_out[part, index * slot_rows:index * slot_rows + kept] = result[:kept]
            if shifted:
                mid_out[part + lag, index * shifted:(index + 1) * shifted] = result[kept:]
            elif index == 0:
                mid_out[part + lag, :middle] = result

    def front(turn, shifted):
        @pl.when(turn < parts)
        def _():
            edge_out[turn] = grad[peer_edge, columns(turn)].astype(low)
            send_edge(turn).start()

        @pl.when(turn >= lag)
        def _():
            send_mid(turn - lag, shifted).wait_recv()

        @pl.when(jnp.logical_and(turn >= lag, turn < parts + lag))
        def _():
            update_middle(turn - lag, shifted)

        @pl.when(turn < lag)
        def _():
            mid_out[turn, :middle] = grad[edge:edge + middle, columns(turn)].astype(low)

        @pl.when(jnp.logical_and(turn >= lag, turn < parts))
        def _():
            mid_out[turn, :middle] = select(
                owns(middle), mid_out[turn, :middle], grad[edge:edge + middle, columns(turn)]).astype(low)

        @pl.when(turn < parts + lag)
        def _():
            send_mid(turn, shifted).start()

        @pl.when(jnp.logical_and(turn >= 1, turn < parts + 1))
        def _():
            update_edge(turn - 1)

        @pl.when(turn >= 2 * lag)
        def _():
            part = turn - 2 * lag
            slot_rows = max(middle - shifted, shifted)
            pieces = [(index * slot_rows, index * shifted, shifted) for index in range(3)]
            for at, come, rows in pieces if shifted else [(0, 0, middle)]:
                slot_out[part, at:at + rows] = select(
                    owns(rows), slot_out[part, at:at + rows],
                    mid_in[turn - lag, come:come + rows]).astype(low)
            send_slot(part, shifted).start()

    load(0).wait()
    each(parts + 2 * lag, front)

    def later(step_of):
        def run(part, carry):
            step_of(part)
            return carry
        lax.fori_loop(deferred, parts, run, 0)

    later(lambda part: send_rest(part).start())

    def arrive(part, shifted):
        slot_rows = max(middle - shifted, shifted)
        def take(rows):
            send_own(part, rows).wait_recv()
            own_in[part, :rows] = select(
                moves(rows), own_in[part, :rows], own_out[part, :rows]).astype(low)

        either(part, take)
        back_out[part, :edge] = own_in[part, :edge]
        send_slot(part, shifted).wait_recv()
        rows = 3 * slot_rows
        slot_in[part, :rows] = select(
            moves(rows), slot_in[part, :rows], slot_out[part, :rows]).astype(low)
        if shifted:
            for index in range(3):
                at = index * shifted
                back_out[part, edge + at:edge + at + shifted] = select(
                    owns_moved(shifted), slot_in[part, at:at + shifted],
                    slot_in[part, index * slot_rows:index * slot_rows + shifted]).astype(low)
        send_back(part, shifted).start()

    def place(part, shifted):
        either(part, functools.partial(place_with, part, shifted))

    def place_with(part, shifted, ready):
        kept = middle - shifted
        slot_rows = max(kept, shifted)
        send_back(part, shifted).wait_recv()
        keeps, last = owns_moved(edge), is_last(edge)
        zero = jnp.zeros((edge, width), high)
        for index in range(3):
            held = slot_in[part, index * slot_rows:index * slot_rows + kept].astype(high)
            if shifted:
                rest = back_in[part, edge + index * shifted:edge + (index + 1) * shifted]
                moved = jnp.concatenate([held, rest.astype(high)], axis=0)
            else:
                moved = held
            ends = zero
            if index * edge < ready:
                ends = own_in[part, index * edge:(index + 1) * edge].astype(high)
            low_half, high_half = moved[:edge], moved[edge:]
            new[part, index, :edge] = jnp.where(
                jnp.logical_and(keeps, last), low_half, ends).astype(low)
            new[part, index, edge:2 * edge] = jnp.where(
                keeps, jnp.where(last, high_half, low_half), zero).astype(low)
            new[part, index, 2 * edge:] = jnp.where(
                keeps, jnp.where(last, ends, high_half), zero).astype(low)
            if index == 0:
                if shifted:
                    other = jnp.concatenate([
                        back_in[part, edge:edge + kept].astype(high),
                        slot_in[part, :shifted].astype(high)], axis=0)
                    moved = jnp.where(owns_moved(middle), moved, other)
                placed[part, edge:edge + middle] = moved.astype(low)
                peer_ends = back_in[part, :edge].astype(high)
                placed[part, :edge] = jnp.where(last, peer_ends, ends).astype(low)
                placed[part, edge + middle:] = jnp.where(last, ends, peer_ends).astype(low)
        if ready > edge:
            store_new(part).start()
        store_placed(part).start()

    def place_rest(part):
        send_rest(part).wait_recv()
        late = jnp.logical_and(owns_moved(edge), is_last(edge))
        for index in (1, 2):
            rows = slice(index * edge, (index + 1) * edge)
            ends = select(moves(edge), own_in[part, rows], own_out[part, rows])
            new[part, index, :edge] = select(late, new[part, index, :edge], ends).astype(low)
            new[part, index, 2 * edge:] = select(
                late, ends, new[part, index, 2 * edge:]).astype(low)
        store_new(part).start()

    def finish(part, shifted):
        send_edge(part).wait_send()
        send_mid(part, shifted).wait_send()
        either(part, lambda rows: send_own(part, rows).wait_send())
        send_slot(part, shifted).wait_send()
        send_back(part, shifted).wait_send()
        store_placed(part).wait()

        @pl.when(part < deferred)
        def _():
            store_new(part).wait()

    def back(turn, shifted):
        @pl.when(turn < parts)
        def _():
            arrive(turn, shifted)

        @pl.when(jnp.logical_and(turn > 0, turn <= parts))
        def _():
            place(turn - 1, shifts[shifts.index(shifted) - 1])

        @pl.when(turn >= trail)
        def _():
            finish(turn - trail, shifted)

    each(parts + trail, back)
    each(lag, lambda part, shifted: send_mid(parts + part, shifted).wait_send())
    later(place_rest)

    def finish_rest(part):
        send_rest(part).wait_send()
        store_new(part).wait()

    later(finish_rest)


def fused(bit, shifts, counts, partner, gradients, master, first, second):
    flat_count, model = gradients.shape
    capacity = master.shape[0]
    edge = flat_count - capacity
    middle = flat_count - 2 * edge
    width, lag = 512, 2
    parts = model // width
    mid_rows = max(max(middle, 3 * shifted) for shifted in shifts)
    slot_rows = max(3 * max(middle - shifted, shifted) for shifted in shifts)
    back_rows = edge + max(
        max(middle - shifted, 3 * shifted) if shifted else 0 for shifted in shifts)
    low, high = jnp.bfloat16, jnp.float32
    sems, more_sems = (pltpu.SemaphoreType.DMA((count,)) for count in (parts, parts + lag))
    smem = pl.BlockSpec(memory_space=pltpu.SMEM)
    anywhere = pl.BlockSpec(memory_space=pl.ANY)

    def pair(count, rows):
        return [pltpu.VMEM((count, rows, width), low)] * 2

    return pl.pallas_call(
        functools.partial(fused_kernel, bit, shifts, lag),
        out_shape=(
            jax.ShapeDtypeStruct((3, capacity, model), low),
            jax.ShapeDtypeStruct((flat_count, model), low),
        ),
        in_specs=[smem, smem] + [anywhere] * 4,
        out_specs=(anywhere, anywhere),
        scratch_shapes=[
            pltpu.VMEM((flat_count, model), high),
            pltpu.VMEM((3, capacity, model), high),
        ] + pair(parts, edge) + pair(parts + lag, mid_rows) + pair(parts, 3 * edge)
        + pair(parts, slot_rows) + pair(parts, back_rows) + [
            pltpu.VMEM((parts, 3, capacity, width), low),
            pltpu.VMEM((parts, flat_count, width), low),
            pltpu.SemaphoreType.DMA((4,)),
        ] + [sems] * 2 + [more_sems] * 2 + [sems] * 10,
        compiler_params=pltpu.CompilerParams(
            collective_id=bit, has_side_effects=True, vmem_limit_bytes=38 * 1024 * 1024),
        name=f"fused_bit_{bit}",
    )(counts, partner, gradients, master, first, second)


def body_pairs(gradients, master_rows, first_moment, second_moment, shard_rows, move_partner):
    bits = lax.axis_size("ep").bit_length() - 1
    moved, placed = lax.switch(
        chosen_case(move_partner),
        [functools.partial(fused, bit, shifts_of_bit[bit]) for bit in range(bits)],
        shard_rows, move_partner, gradients[0], master_rows[0], first_moment[0], second_moment[0],
    )
    wide = moved.astype(jnp.float32)
    return (wide[0][None], wide[1][None], wide[2][None], placed)


def body(gradients, master_rows, first_moment, second_moment, shard_rows, move_partner):
    groups = lax.axis_size("dp")
    capacity = master_rows.shape[1]
    flat_count = gradients.shape[1]
    dp_index = lax.axis_index("dp")
    ep_index = lax.axis_index("ep")
    partner = move_partner[ep_index]
    counts = shard_rows[ep_index]
    moved_counts = shard_rows[partner]
    starts = jnp.cumsum(counts) - counts
    moved_starts = jnp.cumsum(moved_counts) - moved_counts
    own_slots = jnp.arange(capacity, dtype=jnp.int32)
    live = (own_slots < counts[dp_index])[:, None]
    state = jnp.stack([master_rows[0], first_moment[0], second_moment[0]])
    slots = jnp.arange(groups * capacity, dtype=jnp.int32)
    owners = slots // capacity
    within = slots % capacity
    live_all = (within < counts[owners])[:, None]
    source = jnp.minimum(starts[owners] + within, flat_count - 1)
    packed = jnp.where(live_all, jnp.take(gradients[0], source, axis=0), 0.0)
    summed = lax.psum_scatter(
        packed.astype(jnp.bfloat16), "dp", scatter_dimension=0, tiled=True
    ).astype(jnp.float32)
    grad_own = summed / groups
    stepped = jnp.where(live, jnp.stack(adam_step(grad_own, state[0], state[1], state[2])), 0.0)
    moved = move_new(stepped, partner, ep_index, move_partner)
    updated, first_new, second_new = (moved[0], moved[1], moved[2])
    whole = lax.all_gather(updated.astype(jnp.bfloat16), "dp", axis=0, tiled=True)
    flat_rows = jnp.arange(flat_count, dtype=jnp.int32)
    owner_flat = jnp.sum((flat_rows[:, None] >= moved_starts[None, 1:]).astype(jnp.int32), axis=1)
    position = owner_flat * capacity + flat_rows - moved_starts[owner_flat]
    placed = jnp.take(whole, position, axis=0)
    return (updated[None], first_new[None], second_new[None], placed)


def solution(mesh):
    placed = (
        P("dp", "ep", None),
        P("ep", "dp", None),
        P("ep", "dp", None),
        P("ep", "dp", None),
        P(),
        P(),
    )
    return jax.shard_map(
        body_pairs if mesh.shape["dp"] == 2 else body,
        mesh=mesh,
        in_specs=placed,
        out_specs=(P("ep", "dp", None), P("ep", "dp", None), P("ep", "dp", None), P("ep", None)),
        check_vma=False,
    )
```

profile of v0, /device:TPU:0, one launch (start us, length us, event | category | flops | bytes accessed | tf_op | source)
XLA Modules:
  0.0 93.1 jit_solution(17871480031574258391)
XLA Ops:
  0.6 1.3 %xor_reduce_fusion = s32[]{:T(128)} fusion(s32[16]{0:T(128)} %param.15), kind=kLoop, calls=%fused_computation | loop fusion | flops 31 | bytes 68 | tf_op jit(solution)/shard_map/reduce_max | solution.py:35
  3.9 85.3 %conditional.1 = (bf16[128,7168]{1,0:T(8,128)(2,1)S(1)}, f32[1,96,7168]{2,1,0:T(8,128)S(1)}, f32[1,96,7168]{2,1,0:T(8,128)S(1)}, f32[1,96,7168]{2,1,0:T(8,128)S(1)}) conditional(s32[]{:T(128)} %clamp.3, (s32[16,2]{0,1:T(2,128)}, s32[16]{0:T(128)}, f32[128,7168]{1,0:T(8,128)}, f32[96,7168]{1,0:T(8,128)}, ...), branch_computations={%region_1.0_spmd, %region_2.0_spmd, %region_3.0_spmd, %region_4.0_... | conditional | bytes 16515360 | solution.py:405
  3.9 0.8 copy.12.counts_ref
  4.7 83.8 %fused_bit_2.2 = (bf16[3,96,7168]{2,1,0:T(8,128)(2,1)S(1)}, bf16[128,7168]{1,0:T(8,128)(2,1)S(1)}) custom-call(s32[16,2]{1,0:T(8,128)S(1)} %copy.12.counts_ref, s32[16]{0:T(128)} %get-tuple-element.101.partner_ref, f32[128,7168]{1,0:T(8,128)} %get-tuple-element.102.grad_hbm, f32[96,7168]{1,0:T(8,128)} %get-tuple-element.103.master_hbm, ...), custom_call_target="tpu_custom_call" | custom-call | tf_op jit(solution)/shard_map/cond/branch_2_fun/fused_bit_2/pallas_call | solution.py:380
  88.4 0.7 fusion.2
  89.2 0.0 copy-start
  89.2 0.0 copy-start.1
  89.2 0.0 copy-start.2
  89.2 1.3 %copy.31 = bf16[128,7168]{1,0:T(8,128)(2,1)} copy(bf16[128,7168]{1,0:T(8,128)(2,1)S(1)} %get-tuple-element.187) | data formatting | bytes 3670016
  90.5 0.8 copy-done
  91.3 0.9 copy-done.1
  92.2 0.9 copy-done.2
Async XLA Ops:
  89.2 2.1 %copy-start = (f32[1,96,7168]{2,1,0:T(8,128)}, f32[1,96,7168]{2,1,0:T(8,128)S(1)}, u32[]{:S(2)}) copy-start(f32[1,96,7168]{2,1,0:T(8,128)S(1)} %get-tuple-element.186) | copy-start | bytes 8257540
  89.2 3.0 %copy-start.1 = (f32[1,96,7168]{2,1,0:T(8,128)}, f32[1,96,7168]{2,1,0:T(8,128)S(1)}, u32[]{:S(2)}) copy-start(f32[1,96,7168]{2,1,0:T(8,128)S(1)} %get-tuple-element.185) | copy-start | bytes 8257540
  89.2 3.9 %copy-start.2 = (f32[1,96,7168]{2,1,0:T(8,128)}, f32[1,96,7168]{2,1,0:T(8,128)S(1)}, u32[]{:S(2)}) copy-start(f32[1,96,7168]{2,1,0:T(8,128)S(1)} %get-tuple-element.184) | copy-start | bytes 8257540
where the time goes:
time: 93.3 us; the launch traced here: 93.1 us
  Pallas kernels  83.8 us (90%)
  local copies, waits for them, and re-layouts  5.37 us (6%)
  between operations  2.61 us (3%)
  other arithmetic  1.29 us (1%)
    pallas_call x1, Pallas kernels, fused(): pl.pallas_call(functools.partial(fused_kernel, bit, shifts, lag), out_sha...  83.8 us
    unnamed x7, local copies, waits for them, and re-layouts  3.87 us

commit v1 on v0

--- a/solution.py
+++ b/solution.py
@@ -363,7 +363,7 @@
     capacity = master.shape[0]
     edge = flat_count - capacity
     middle = flat_count - 2 * edge
-    width, lag = 512, 2
+    width, lag = 512, 4
     parts = model // width
     mid_rows = max(max(middle, 3 * shifted) for shifted in shifts)
     slot_rows = max(3 * max(middle - shifted, shifted) for shifted in shifts)

time: 93.3 us -> 96.9 us (1.039)
  Pallas kernels: 83.8 us -> 87.4 us
    pallas_call x1, Pallas kernels: 83.8 us -> 87.4 us  [fused(): pl.pallas_call(functools.partial(fused_kernel, bit, shifts, lag), out_sha...]
where the time goes in v1:
time: 96.9 us; the launch traced here: 96.7 us
  Pallas kernels  87.4 us (90%)
  local copies, waits for them, and re-layouts  5.37 us (6%)
  between operations  2.61 us (3%)
  other arithmetic  1.29 us (1%)
    pallas_call x1, Pallas kernels, fused(): pl.pallas_call(functools.partial(fused_kernel, bit, shifts, lag), out_sha...  87.4 us
    unnamed x7, local copies, waits for them, and re-layouts  3.87 us

profile of v1, /device:TPU:0, one launch (start us, length us, event | category | flops | bytes accessed | tf_op | source)
XLA Modules:
  0.0 96.7 jit_solution(5002934873204476552)
XLA Ops:
  0.6 1.3 %xor_reduce_fusion = s32[]{:T(128)} fusion(s32[16]{0:T(128)} %param.15), kind=kLoop, calls=%fused_computation | loop fusion | flops 31 | bytes 68 | tf_op jit(solution)/shard_map/reduce_max | solution.py:35
  3.9 88.9 %conditional.1 = (bf16[128,7168]{1,0:T(8,128)(2,1)S(1)}, f32[1,96,7168]{2,1,0:T(8,128)S(1)}, f32[1,96,7168]{2,1,0:T(8,128)S(1)}, f32[1,96,7168]{2,1,0:T(8,128)S(1)}) conditional(s32[]{:T(128)} %clamp.3, (s32[16,2]{0,1:T(2,128)}, s32[16]{0:T(128)}, f32[128,7168]{1,0:T(8,128)}, f32[96,7168]{1,0:T(8,128)}, ...), branch_computations={%region_1.0_spmd, %region_2.0_spmd, %region_3.0_spmd, %region_4.0_... | conditional | bytes 16515360 | solution.py:405
  3.9 0.8 copy.11.counts_ref
  4.7 87.4 %fused_bit_1.2 = (bf16[3,96,7168]{2,1,0:T(8,128)(2,1)S(1)}, bf16[128,7168]{1,0:T(8,128)(2,1)S(1)}) custom-call(s32[16,2]{1,0:T(8,128)S(1)} %copy.11.counts_ref, s32[16]{0:T(128)} %get-tuple-element.93.partner_ref, f32[128,7168]{1,0:T(8,128)} %get-tuple-element.94.grad_hbm, f32[96,7168]{1,0:T(8,128)} %get-tuple-element.95.master_hbm, ...), custom_call_target="tpu_custom_call" | custom-call | tf_op jit(solution)/shard_map/cond/branch_1_fun/fused_bit_1/pallas_call | solution.py:380
  92.0 0.7 fusion.1
  92.8 0.0 copy-start
  92.8 0.0 copy-start.1
  92.8 0.0 copy-start.2
  92.8 1.3 %copy.31 = bf16[128,7168]{1,0:T(8,128)(2,1)} copy(bf16[128,7168]{1,0:T(8,128)(2,1)S(1)} %get-tuple-element.187) | data formatting | bytes 3670016
  94.1 0.8 copy-done
  94.9 0.9 copy-done.1
  95.8 0.9 copy-done.2
Async XLA Ops:
  92.8 2.1 %copy-start = (f32[1,96,7168]{2,1,0:T(8,128)}, f32[1,96,7168]{2,1,0:T(8,128)S(1)}, u32[]{:S(2)}) copy-start(f32[1,96,7168]{2,1,0:T(8,128)S(1)} %get-tuple-element.186) | copy-start | bytes 8257540
  92.8 3.0 %copy-start.1 = (f32[1,96,7168]{2,1,0:T(8,128)}, f32[1,96,7168]{2,1,0:T(8,128)S(1)}, u32[]{:S(2)}) copy-start(f32[1,96,7168]{2,1,0:T(8,128)S(1)} %get-tuple-element.185) | copy-start | bytes 8257540
  92.8 3.9 %copy-start.2 = (f32[1,96,7168]{2,1,0:T(8,128)}, f32[1,96,7168]{2,1,0:T(8,128)S(1)}, u32[]{:S(2)}) copy-start(f32[1,96,7168]{2,1,0:T(8,128)S(1)} %get-tuple-element.184) | copy-start | bytes 8257540
